TPU v7x, 256 devices: a whole 4x4x8 slice. The times are simulated.
256 devices in a mesh: poke: 32 (over z_hi, x, y), sensor: 8 (over z_lo, core).
Axes of the slice: x: 4, y: 4, z: 8 (z_hi: 2, z_lo: 4; z = z_hi * 4 + z_lo), core: 2. Of those that a mesh axis runs over, the one named last changes fastest.
Arguments:
- push_slopes: bfloat16 [8192, 6, 8192], P('poke', None, 'sensor'), may hold values from -6 to 6
- pull_slopes: bfloat16 [8192, 6, 8192], P('poke', None, 'sensor'), may hold values from -6 to 6
- pattern_order: int32 [256], replicated, may hold values from 0 to 255, each once
- star_map: int32 [6, 8192], P(None, 'sensor'), may hold values from 0 to 8191, as said below
Outputs:
- gram_matrix: float32 [8192, 8192], P('poke', 'sensor')
Inputs may be any that keep to these rules, and one draw needn't show every extreme that they name: `pattern_order`: a permutation of 0 to 255. `star_map`: each row is a permutation of 0 to 8191 that keeps every index within its aligned block of 1024 slopes.
All inputs are finite; a program needn't handle non-finite values.
Results may differ from a plain program's by a relative error of at most 0.0042.
Values may be sent and summed in bfloat16 or wider, within the bound.
A program may use at most 128 MiB of HBM per device.

v0:
```python
import math

import jax
import jax.numpy as jnp
from jax import lax
from jax.sharding import PartitionSpec as P


def sign_table(first_index, second_index, bit_count):
    masked = jnp.bitwise_and(first_index[:, None], second_index[None, :])
    parity = jnp.zeros(masked.shape, jnp.int32)
    for shift_bits in range(bit_count):
        parity = parity + jnp.bitwise_and(jnp.right_shift(masked, shift_bits), 1)
    return (1 - 2 * (parity % 2)).astype(jnp.float32)


def star_average(values, local_map, star_count):
    summed = jnp.take(values[:, 0, :], local_map[0], axis=1).astype(jnp.float32)
    for star_index in range(1, star_count):
        summed = summed + jnp.take(values[:, star_index, :], local_map[star_index], axis=1).astype(
            jnp.float32
        )
    return summed / star_count


def local(push_slopes, pull_slopes, pattern_order, star_map):
    frames_dev = pattern_order.shape[0]
    star_count = push_slopes.shape[1]
    slopes_dev = push_slopes.shape[2]
    poke_count = lax.axis_size("poke")
    sensor_count = lax.axis_size("sensor")
    frame_total = frames_dev * poke_count
    modes_dev = frames_dev // poke_count
    sign_local = sign_table(
        jnp.arange(frames_dev, dtype=jnp.int32), pattern_order, frames_dev.bit_length()
    )
    across_index = jnp.arange(poke_count, dtype=jnp.int32)
    sign_across = sign_table(across_index, across_index, poke_count.bit_length())
    local_map = star_map % slopes_dev
    difference = (push_slopes.astype(jnp.float32) - pull_slopes.astype(jnp.float32)).astype(
        jnp.bfloat16
    )
    averaged_frames = star_average(difference, local_map, star_count)
    transformed = jnp.dot(sign_local, averaged_frames, precision=lax.Precision.HIGHEST)
    stacked = transformed.reshape(1, poke_count, modes_dev, slopes_dev)
    mixed_modes = jnp.einsum(
        "la,aonw->nlw",
        sign_across,
        lax.all_to_all(stacked, "poke", split_axis=1, concat_axis=0, tiled=True),
        precision=lax.Precision.HIGHEST,
    )
    averaged = mixed_modes.reshape(frames_dev, slopes_dev)
    demodulated = (averaged / math.sqrt(frame_total)).astype(jnp.bfloat16)
    slope_total = slopes_dev * sensor_count
    partial_value = lax.dot_general(
        demodulated,
        lax.all_gather(demodulated, "poke", axis=0, tiled=True),
        (((1,), (1,)), ((), ())),
        preferred_element_type=jnp.float32,
    )
    gram_block = lax.psum_scatter(partial_value, "sensor", scatter_dimension=1, tiled=True)
    return gram_block / math.sqrt(slope_total)


def solution(mesh):
    return jax.shard_map(
        local,
        mesh=mesh,
        in_specs=(P("poke", None, "sensor"), P("poke", None, "sensor"), P(), P(None, "sensor")),
        out_specs=P("poke", "sensor"),
        check_vma=False,
    )
```

profile of v0, /device:TPU:65, one launch (start us, length us, event | category | flops | bytes accessed | tf_op | source)
XLA Modules:
  0.0 446.6 jit_solution(10072445940244133799)
XLA Ops:
  6.5 0.8 add_select_fusion.1
  7.5 3.2 copy.8
  10.7 4.7 %copy.9 = bf16[256,6,1024]{0,2,1:T(8,128)(2,1)} copy(bf16[256,6,1024]{2,0,1:T(8,128)(2,1)} %param.7) | data formatting | bytes 6291456 | tf_op args[1]
  15.3 2.6 subtract_convert_fusion
  18.0 0.2 slice_bitcast_fusion.5
  18.2 5.0 %gather_fusion = bf16[1024,256]{1,0:T(8,128)(2,1)} fusion(bf16[256,1024]{0,1:T(8,128)(2,1)S(1)} %get-tuple-element.6, s32[1024]{0:T(1024)S(1)} %fusion.69), kind=kCustom, calls=%fused_computation.clone | custom fusion | bytes 1052672 | tf_op jit(solution)/shard_map/jit(_take)/gather | solution.py:18
  23.1 3.9 gather_fusion.5
  27.1 3.9 gather_fusion.4
  31.0 0.0 copy-start
  31.0 0.0 copy-start.2
  31.0 5.0 %gather_fusion.3 = bf16[1024,256]{1,0:T(8,128)(2,1)} fusion(bf16[256,1024]{0,1:T(8,128)(2,1)S(1)} %get-tuple-element.9, s32[1024]{0:T(1024)S(1)} %fusion.72), kind=kCustom, calls=%fused_computation.3.clone | custom fusion | bytes 1052672 | tf_op jit(solution)/shard_map/jit(_take)/gather | solution.py:20
  36.0 4.9 %gather_fusion.2 = bf16[1024,256]{1,0:T(8,128)(2,1)} fusion(bf16[256,1024]{0,1:T(8,128)(2,1)S(1)} %get-tuple-element.10, s32[1024]{0:T(1024)S(1)} %fusion.71), kind=kCustom, calls=%fused_computation.2.clone | custom fusion | bytes 1052672 | tf_op jit(solution)/shard_map/jit(_take)/gather | solution.py:20
  41.0 3.9 gather_fusion.1
  44.9 0.0 copy-done
  44.9 3.2 convolution_bitcast_fusion
  48.2 41.8 %all_to_all.4 = f32[1,32,8,1024]{3,2,0,1:T(8,128)S(1)} all-to-all(f32[1,32,8,1024]{3,2,0,1:T(8,128)S(1)} %convolution_bitcast_fusion), channel_id=1, replica_groups=mesh['poke'=32,'sensor'=8] {'poke'}, dimensions={1} | all-to-all | bytes 2097152 | tf_op jit(solution)/shard_map/all_to_all | solution.py:49
  90.0 2.5 fusion
  92.5 0.0 all-gather.2.cloned.1.call-update
  92.5 0.2 reduce-scatter.2.cloned.1.call-start
  92.7 238.1 %all-gather.2.cloned.1.call-done = bf16[8192,1024]{1,0:T(8,128)(2,1)} async-done(((bf16[256,1024]{1,0:T(8,128)(2,1)}), bf16[8192,1024]{1,0:T(8,128)(2,1)}) %all-gather.2.cloned.1.call-update) | async-done | bytes 16777232 | tf_op jit(solution)/shard_map/all_gather | solution.py:57
  330.8 13.7 %fusion.93 = f32[256,8192]{1,0:T(8,128)} fusion(bf16[256,1024]{1,0:T(8,128)(2,1)} %bitcast.64, bf16[8192,1024]{1,0:T(8,128)(2,1)} %all-gather.2.cloned.1.call-done), kind=kOutput, calls=%fused_computation.128 | convolution fusion | flops 4294967296 | bytes 25690112 | tf_op jit(solution)/shard_map/dot_general | solution.py:55
  344.5 0.0 reduce-scatter.2.cloned.1.call-update
  344.5 92.9 %reduce-scatter.2.cloned.1.call-done = f32[256,1024]{1,0:T(8,128)} async-done(((f32[256,8192]{1,0:T(8,128)}), f32[256,1024]{1,0:T(8,128)}) %reduce-scatter.2.cloned.1.call-update) | async-done | bytes 1048592 | tf_op jit(solution)/shard_map/reduce_scatter | solution.py:61
  437.4 2.3 broadcast_multiply_fusion
  (14 shorter events, 0.1 us)
Async XLA Ops:
  6.5 324.2 %all-gather.2.cloned.1.call-start = ((), (), s32[]{:S(2)}) async-start(), calls=%async_computation.2 | async-start | bytes 17301504 | tf_op jit(solution)/shard_map/all_gather | solution.py:57
  31.0 13.9 %copy-start = (bf16[1024,256]{1,0:T(8,128)(2,1)S(1)}, bf16[1024,256]{1,0:T(8,128)(2,1)}, u32[]{:S(2)}) copy-start(bf16[1024,256]{1,0:T(8,128)(2,1)} %gather_fusion) | copy-start | bytes 1572868
  31.0 13.9 %copy-start.2 = (s32[256]{0:T(256)S(1)}, s32[256]{0:T(256)}, u32[]{:S(2)}) copy-start(s32[256]{0:T(256)} %param.8) | copy-start | bytes 3076
  36.0 8.9 %copy-start.1 = (bf16[1024,256]{1,0:T(8,128)(2,1)S(1)}, bf16[1024,256]{1,0:T(8,128)(2,1)}, u32[]{:S(2)}) copy-start(bf16[1024,256]{1,0:T(8,128)(2,1)} %gather_fusion.3) | copy-start | bytes 1572868
  92.5 344.9 %reduce-scatter.2.cloned.1.call-start = ((), (), s32[]{:S(2)}) async-start(), calls=%async_computation.3 | async-start | bytes 9437184 | tf_op jit(solution)/shard_map/reduce_scatter | solution.py:61
Sparse Core Ops, SparseCore 0:
  92.6 238.1 all-gather.1
  344.6 92.7 reduce-scatter.1
where the time goes:
time: 450 us; the launch traced here: 447 us
  waiting for transfers between devices  331 us (74%)
  blocking collectives  41.8 us (9%)
  local copies, waits for them, and re-layouts  34.8 us (8%)
  matrix products  19.4 us (4%)
  between operations  13.6 us (3%)
  other arithmetic  5.81 us (1%)
    all_gather x1, waiting for transfers between devices, local(): lax.all_gather(demodulated, 'poke', axis=0, tiled=True)  238 us
    reduce_scatter x1, waiting for transfers between devices, local(): lax.psum_scatter(partial_value, 'sensor', scatter_dimension=1, tiled=True)  92.9 us
    all_to_all x1, blocking collectives, local(): lax.all_to_all(stacked, 'poke', split_axis=1, concat_axis=0, tiled=True)  41.8 us
    gather x5, local copies, waits for them, and re-layouts, star_average(): jnp.take(values[:, star_index, :], local_map[star_index], axis=1)  21.7 us
    dot_general x1, matrix products, local(): lax.dot_general(demodulated, lax.all_gather(demodulated, 'poke', axis=0,...  13.7 us
  transfers between devices with their start and end apart: 2, of which 2 were waited for; matrix products, arithmetic and copies ran while one was open for 0% of the time, Pallas kernels for 0%

commit v1 on v0

v1 whole, which is shorter than its diff:
```python
import functools
import math

import jax
import jax.numpy as jnp
from jax import lax
from jax.experimental import pallas as pl
from jax.experimental.pallas import tpu as pltpu
from jax.sharding import PartitionSpec as P

MESH = pl.DeviceIdType.MESH
STARS, FRAMES, SLOPES = 6, 256, 1024
HALF = SLOPES // 2
ROWS = 512
KEPT = 5
F32, BF16 = jnp.float32, jnp.bfloat16


def parity(bits):
    for shift in (4, 2, 1):
        bits = bits ^ (bits >> shift)
    return bits & 1


def star_kernel(push_ref, pull_ref, order_ref, map_ref, t_ref, total):
    star = pl.program_id(0)
    difference = (push_ref[0].astype(F32) - pull_ref[0].astype(F32)).astype(BF16)
    index = map_ref[pl.ds(star, 1), :] % SLOPES
    hot = (lax.broadcasted_iota(jnp.int32, (SLOPES, SLOPES), 0) == index).astype(F32).astype(BF16)
    part = jnp.dot(difference, hot, preferred_element_type=F32)

    @pl.when(star == 0)
    def _():
        total[...] = part

    @pl.when(star > 0)
    def _():
        total[...] += part

    @pl.when(star == STARS - 1)
    def _():
        averaged = total[...] / STARS
        high = averaged.astype(BF16)
        low = (averaged - high.astype(F32)).astype(BF16)
        row = lax.broadcasted_iota(jnp.int32, (FRAMES, FRAMES), 0)
        mode = (row // 8 % 2) * 128 + (row // 16) * 8 + row % 8
        sign = (1 - 2 * parity(mode & order_ref[...])).astype(F32).astype(BF16)
        t = jnp.dot(sign, high, preferred_element_type=F32)
        t += jnp.dot(sign, low, preferred_element_type=F32)
        t_ref[0] = t[:, :HALF].astype(t_ref.dtype)
        t_ref[1] = t[:, HALF:].astype(t_ref.dtype)


def star_stage(push, pull, order, star_map):
    return pl.pallas_call(
        star_kernel,
        out_shape=jax.ShapeDtypeStruct((2, FRAMES, HALF), BF16),
        grid=(STARS,),
        in_specs=[
            pl.BlockSpec((1, FRAMES, SLOPES), lambda g: (g, 0, 0)),
            pl.BlockSpec((1, FRAMES, SLOPES), lambda g: (g, 0, 0)),
            pl.BlockSpec((1, FRAMES), lambda g: (0, 0)),
            pl.BlockSpec((STARS, SLOPES), lambda g: (0, 0)),
        ],
        out_specs=pl.BlockSpec((2, FRAMES, HALF), lambda g: (0, 0, 0)),
        scratch_shapes=[pltpu.VMEM((FRAMES, SLOPES), F32)],
        compiler_params=pltpu.CompilerParams(vmem_limit_bytes=48 * 2**20),
        name="star_stage",
    )(jnp.transpose(push, (1, 0, 2)), jnp.transpose(pull, (1, 0, 2)), order.reshape(1, -1), star_map)


def device(zh, x, y, zl, c):
    return (zh * 16 + x * 4 + y, zl * 2 + c)


def offsets(k):
    return k % 3 + (k // 9) * 3, (k // 3) % 3 + k // 9


def gram_kernel(
    t_ref,
    out_ref,
    mixed,
    row_block,
    col_block,
    pair_out,
    pair_in,
    part,
    ring_out,
    ring_in,
    final,
    final_t,
    mix_send,
    mix_recv,
    gather_send,
    gather_recv,
    pair_send,
    pair_recv,
    ring_send,
    ring_recv,
    final_send,
    final_recv,
):
    poke, sensor = lax.axis_index("poke"), lax.axis_index("sensor")
    zh, x, y = poke // 16, (poke // 4) % 4, poke % 4
    zl, c = sensor // 2, sensor % 2
    z = zh * 4 + zl

    def remote(src, dst, send, recv, target):
        return pltpu.make_async_remote_copy(
            src_ref=src, dst_ref=dst, send_sem=send, recv_sem=recv, device_id=target, device_id_type=MESH
        )

    def mix_copy(o):
        zh2, x2, y2 = (zh + 1 - o // 16) % 2, (x + (o // 4) % 4) % 4, (y + o % 4) % 4
        rows = pl.multiple_of(16 * (4 * x2 + y2), 16)
        return remote(
            t_ref.at[zh2, pl.ds(rows, 16)],
            mixed.at[pl.ds(pl.multiple_of(16 * poke, 16), 16)],
            mix_send.at[o],
            mix_recv.at[o],
            device(zh2, x2, y2, zl, c),
        )

    lax.fori_loop(0, 16, lambda o, _: (mix_copy(o).start(), 0)[1], 0)
    lax.fori_loop(17, 32, lambda o, _: (mix_copy(o).start(), 0)[1], 0)
    mixed[pl.ds(pl.multiple_of(16 * poke, 16), 16), :] = t_ref[
        zh, pl.ds(pl.multiple_of(16 * (4 * x + y), 16), 16), :
    ]
    row = lax.broadcasted_iota(jnp.int32, (ROWS, ROWS), 0)
    col = lax.broadcasted_iota(jnp.int32, (ROWS, ROWS), 1)
    sign = 1 - 2 * parity((row % 32) & (col // 16))
    sign = jnp.where(row // 32 == col % 16, sign, 0).astype(F32).astype(BF16)
    lax.fori_loop(0, 16, lambda o, _: (mix_copy(o).wait(), 0)[1], 0)
    lax.fori_loop(17, 32, lambda o, _: (mix_copy(o).wait(), 0)[1], 0)
    demodulated = jnp.dot(sign, mixed[...], preferred_element_type=F32)
    demodulated = (demodulated * (1.0 / math.sqrt(8192))).astype(BF16)
    row_block[0] = demodulated
    col_block[0] = demodulated

    gathers = []
    for d in (1, 2):
        target = device(zh, x, (y + 4 - d) % 4, zl, c)
        gathers.append(remote(row_block.at[0], row_block.at[d], gather_send.at[d], gather_recv.at[d], target))
    for d in (1, 2, 3):
        target = device(zh, (x + 4 - d) % 4, y, zl, c)
        gathers.append(
            remote(col_block.at[0], col_block.at[d], gather_send.at[2 + d], gather_recv.at[2 + d], target)
        )
    for copy in gathers:
        copy.start()
    for copy in gathers:
        copy.wait()

    def block(k):
        dx, dy = offsets(k)
        return lax.dot_general(
            row_block[dy], col_block[dx], (((1,), (1,)), ((), ())), preferred_element_type=F32
        )

    def pair_copy(kk):
        return remote(
            pair_out.at[kk], pair_in.at[kk], pair_send.at[kk], pair_recv.at[kk], device(zh, x, y, zl, 1 - c)
        )

    def give(kk, _):
        pair_out[kk] = block((1 - c) * KEPT + kk).astype(BF16)
        pair_copy(kk).start()
        return 0

    def keep(kk, _):
        value = block(c * KEPT + kk)
        pair_copy(kk).wait()
        value += pair_in[kk].astype(F32)
        for j in range(8):
            r, s = (j // 4) * 256 + (j % 2) * 128, (j // 2 % 2) * 256
            part[j, kk] = value[r : r + 128, s : s + 256]
        return 0

    lax.fori_loop(0, KEPT, give, 0)
    lax.fori_loop(0, KEPT, keep, 0)

    def ring_copy(way, d, half):
        z2 = (z + (1 if way == 0 else 7)) % 8
        return remote(
            ring_out.at[way, d, half],
            ring_in.at[way, d, half],
            ring_send.at[way, d, half],
            ring_recv.at[way, d, half],
            device(z2 // 4, x, y, z2 % 4, c),
        )

    def ring_step(way, d, half, first):
        chunk = (z + (d if way == 0 else 8 - d)) % 8
        value = part[chunk, :, half * 64 : half * 64 + 64, :]
        if not first:
            ring_copy(way, d, half).wait_recv()
            value = value + ring_in[way, d, half].astype(F32)
        ring_out[way, d - 1, half] = value.astype(BF16)
        ring_copy(way, d - 1, half).start()

    ring_step(0, 4, 0, True)
    ring_step(1, 4, 1, True)
    ring_step(0, 3, 1, True)
    ring_step(1, 3, 0, True)
    for d in (3, 2, 1):
        ring_step(0, d, 0, False)
        ring_step(1, d, 1, False)
        if d > 1:
            ring_step(0, d - 1, 1, False)
            ring_step(1, d - 1, 0, False)
    for way in (0, 1):
        for half in (0, 1):
            ring_copy(way, 0, half).wait_recv()
    for half in (0, 1):
        rows = slice(half * 64, half * 64 + 64)
        value = part[z, :, rows, :] + ring_in[0, 0, half].astype(F32) + ring_in[1, 0, half].astype(F32)
        final[:, rows, :] = value * (1.0 / math.sqrt(8192))

    zz2, b = zl // 2, zl % 2

    def ship(src, dst, send, recv, target):
        here = (target[0] == poke) & (target[1] == sensor)

        @pl.when(here)
        def _():
            pltpu.make_async_copy(src, dst, recv).start()

        @pl.when(jnp.logical_not(here))
        def _():
            remote(src, dst, send, recv, target).start()

        return here

    def shipped(src, dst, send, recv, target):
        @pl.when(jnp.logical_not((target[0] == poke) & (target[1] == sensor)))
        def _():
            remote(src, dst, send, recv, target).wait_send()

    def direct(kk):
        dx, dy = offsets(c * KEPT + kk)
        i, j = (x + dx) % 4, (y + dy) % 4
        dst = out_ref.at[pl.ds(pl.multiple_of(b * 128, 128), 128), pl.ds(pl.multiple_of(y * 256, 256), 256)]
        return (
            final.at[kk],
            dst,
            final_send.at[0, kk],
            final_recv.at[y, b],
            device(zh, x, j, 2 * zz2 + i // 2, i % 2),
        )

    def mirrored(kk):
        dx, dy = offsets(c * KEPT + kk)
        i, j = (x + dx) % 4, (y + dy) % 4
        dst = out_ref.at[:, pl.ds(pl.multiple_of(j * 256 + b * 128, 128), 128)]
        return (
            final_t.at[kk],
            dst,
            final_send.at[1, kk],
            final_recv.at[j, b],
            device(zz2, i, y, 2 * zh + x // 2, x % 2),
        )

    def has_mirror(kk):
        k = c * KEPT + kk
        return (k % 2 == 1) | (k == 4)

    for kk in range(KEPT):
        ship(*direct(kk))
    for kk in range(KEPT):

        @pl.when(has_mirror(kk))
        def _():
            final_t[kk] = final[kk].T
            ship(*mirrored(kk))

    for j in range(4):
        for half in range(2):
            pltpu.make_async_copy(final.at[0], out_ref.at[0:128, 0:256], final_recv.at[j, half]).wait()
    for kk in range(KEPT):
        shipped(*direct(kk))

        @pl.when(has_mirror(kk))
        def _():
            shipped(*mirrored(kk))

    for d in (3, 2, 1, 0):
        for way in (0, 1):
            for half in (0, 1):
                if d < 3 or way == half:
                    ring_copy(way, d, half).wait_send()


def gram_stage(t):
    dma = pltpu.SemaphoreType.DMA
    return pl.pallas_call(
        gram_kernel,
        out_shape=jax.ShapeDtypeStruct((256, 1024), F32),
        in_specs=[pl.BlockSpec(memory_space=pltpu.VMEM)],
        out_specs=pl.BlockSpec(memory_space=pltpu.VMEM),
        scratch_shapes=[
            pltpu.VMEM((ROWS, HALF), BF16),
            pltpu.VMEM((3, ROWS, HALF), BF16),
            pltpu.VMEM((4, ROWS, HALF), BF16),
            pltpu.VMEM((KEPT, ROWS, ROWS), BF16),
            pltpu.VMEM((KEPT, ROWS, ROWS), BF16),
            pltpu.VMEM((8, KEPT, 128, 256), F32),
            pltpu.VMEM((2, 4, 2, KEPT, 64, 256), BF16),
            pltpu.VMEM((2, 4, 2, KEPT, 64, 256), BF16),
            pltpu.VMEM((KEPT, 128, 256), F32),
            pltpu.VMEM((KEPT, 256, 128), F32),
            dma((32,)),
            dma((32,)),
            dma((6,)),
            dma((6,)),
            dma((KEPT,)),
            dma((KEPT,)),
            dma((2, 4, 2)),
            dma((2, 4, 2)),
            dma((2, KEPT)),
            dma((4, 2)),
        ],
        compiler_params=pltpu.CompilerParams(has_side_effects=True, vmem_limit_bytes=48 * 2**20),
        name="gram_stage",
    )(t)


def local(push_slopes, pull_slopes, pattern_order, star_map):
    return gram_stage(star_stage(push_slopes, pull_slopes, pattern_order, star_map))


def solution(mesh):
    return jax.shard_map(
        local,
        mesh=mesh,
        in_specs=(P("poke", None, "sensor"), P("poke", None, "sensor"), P(), P(None, "sensor")),
        out_specs=P("poke", "sensor"),
        check_vma=False,
    )
```

time: 450 us -> 130 us (0.29)
  waiting for transfers between devices: 331 us -> 0 us
  Pallas kernels: 0 us -> 126 us
  blocking collectives: 41.8 us -> 0 us
  local copies, waits for them, and re-layouts: 34.8 us -> 4.3 us
  matrix products: 19.4 us -> 0 us
  between operations: 13.6 us -> 0.02 us
  other arithmetic: 5.81 us -> 0 us
    all_gather x1 -> x0, waiting for transfers between devices: 238 us -> none  [local(): lax.all_gather(demodulated, 'poke', axis=0, tiled=True)]
    pallas_call x0 -> x2, Pallas kernels: none -> 126 us  [the longest x1 118 us: gram_stage(): pl.pallas_call(gram_kernel, out_shape=jax.ShapeDtypeStruct((256, 1024), F...]
    reduce_scatter x1 -> x0, waiting for transfers between devices: 92.9 us -> none  [local(): lax.psum_scatter(partial_value, 'sensor', scatter_dimension=1, tiled=True)]
    all_to_all x1 -> x0, blocking collectives: 41.8 us -> none  [local(): lax.all_to_all(stacked, 'poke', split_axis=1, concat_axis=0, tiled=True)]
    gather x6 -> x0, local copies, waits for them, and re-layouts: 26.7 us -> none  [the longest x5 21.7 us: star_average(): jnp.take(values[:, star_index, :], local_map[star_index], axis=1)]
    dot_general x3 -> x0, matrix products: 19.4 us -> none  [the longest x1 13.7 us: local(): lax.dot_general(demodulated, lax.all_gather(demodulated, 'poke', axis=0,...]
  transfers between devices with their start and end apart: 2 -> 0, of which waited for: 2 -> 0; matrix products, arithmetic and copies ran while one was open for 0% -> 0% of each run, Pallas kernels for 0% -> 0%
where the time goes in v1:
time: 130 us
  Pallas kernels  126 us (97%)
  local copies, waits for them, and re-layouts  4.3 us (3%)
    pallas_call x1, Pallas kernels, gram_stage(): pl.pallas_call(gram_kernel, out_shape=jax.ShapeDtypeStruct((256, 1024), F...  118 us
    pallas_call x1, Pallas kernels, star_stage(): pl.pallas_call(star_kernel, out_shape=jax.ShapeDtypeStruct((2, FRAMES, HA...  7.39 us
    unnamed x7, local copies, waits for them, and re-layouts  4.3 us

profile of v1, /device:TPU:65, one launch (start us, length us, event | category | flops | bytes accessed | tf_op | source)
XLA Modules:
  0.0 130.0 jit_solution(15941093368353325139)
XLA Ops:
  0.0 0.0 copy-start
  0.0 1.9 %copy-done = bf16[256,6,1024]{2,0,1:T(8,128)(2,1)S(1)} copy-done((bf16[256,6,1024]{2,0,1:T(8,128)(2,1)S(1)}, bf16[256,6,1024]{2,0,1:T(8,128)(2,1)}, u32[]{:S(2)}) %copy-start) | copy-done | bytes 3145752
  1.9 0.0 copy-start.1
  1.9 0.8 copy-done.1
  2.6 0.0 copy-start.2
  2.7 0.7 copy-done.2
  3.3 7.4 %star_stage.1.t_ref = bf16[2,256,512]{2,1,0:T(8,128)(2,1)S(1)} custom-call(bf16[6,256,1024]{2,1,0:T(8,128)(2,1)S(1)} %bitcast.3, bf16[6,256,1024]{2,1,0:T(8,128)(2,1)} %bitcast.5, s32[1,256]{1,0:T(1,128)S(1)} %bitcast.4, s32[6,1024]{1,0:T(8,128)S(1)} %copy-done.1), custom_call_target="tpu_custom_call" | custom-call | tf_op jit(solution)/shard_map/star_stage/pallas_call | solution.py:55
  10.7 118.3 %gram_stage.1 = f32[256,1024]{1,0:T(8,128)S(1)} custom-call(bf16[2,256,512]{2,1,0:T(8,128)(2,1)S(1)} %star_stage.1.t_ref), custom_call_target="tpu_custom_call" | custom-call | tf_op jit(solution)/shard_map/gram_stage/pallas_call | solution.py:296
  129.1 1.0 copy.6
Async XLA Ops:
  0.0 1.9 %copy-start = (bf16[256,6,1024]{2,0,1:T(8,128)(2,1)S(1)}, bf16[256,6,1024]{2,0,1:T(8,128)(2,1)}, u32[]{:S(2)}) copy-start(bf16[256,6,1024]{2,0,1:T(8,128)(2,1)} %param.4) | copy-start | bytes 9437188
  1.9 0.8 copy-start.1
  2.6 0.7 copy-start.2

commit v2 on v0

v2 whole, which is shorter than its diff:
```python
import functools
import math

import jax
import jax.numpy as jnp
from jax import lax
from jax.experimental import pallas as pl
from jax.experimental.pallas import tpu as pltpu
from jax.sharding import PartitionSpec as P

MESH = pl.DeviceIdType.MESH
STARS, FRAMES, SLOPES = 6, 256, 1024
HALF = SLOPES // 2
ROWS = 512
KEPT = 5
F32, BF16 = jnp.float32, jnp.bfloat16
SENT = BF16
PIECES = 2
WIDTH = HALF // PIECES


def parity(bits):
    for shift in (4, 2, 1):
        bits = bits ^ (bits >> shift)
    return bits & 1


def device(zh, x, y, zl, c):
    return (zh * 16 + x * 4 + y, zl * 2 + c)


BLOCKS = (((0, 0), (0, 1), (3, 1), (0, 2), (1, 2)), ((1, 0), (1, 1), (2, 0), (2, 1), (2, 2)))


GROUPS = ((0, 1), (1, 2), (2, 3), (3, 4), (4, 5))


def is_computed(dx, dy):
    return jnp.where(((dx < 3) & (dy < 3)) | ((dx == 3) & (dy == 1)), 1, 0)


def is_mirrored(dx, dy):
    return (dx % 2, dy % 2) != (0, 0)


def demodulation_kernel(
    push_ref,
    pull_ref,
    order_hbm,
    map_hbm,
    out_ref,
    push,
    pull,
    order_ref,
    map_ref,
    difference,
    total,
    transformed,
    mixed,
    row_block,
    col_block,
    pair_out,
    pair_in,
    part,
    ring_out,
    ring_in,
    final_out,
    final_in,
    load_sem,
    table_sem,
    mix_send,
    mix_recv,
    gather_send,
    gather_recv,
    pair_send,
    pair_recv,
    ring_send,
    ring_recv,
    final_send,
    final_recv,
):
    poke, sensor = lax.axis_index("poke"), lax.axis_index("sensor")
    zh, x, y = poke // 16, (poke // 4) % 4, poke % 4
    zl, c = sensor // 2, sensor % 2
    z = zh * 4 + zl
    zz2, b = zl // 2, zl % 2

    def remote(src, dst, send, recv, target):
        return pltpu.make_async_remote_copy(
            src_ref=src, dst_ref=dst, send_sem=send, recv_sem=recv, device_id=target, device_id_type=MESH
        )

    def load(star):
        return (
            pltpu.make_async_copy(push_ref.at[star], push.at[star], load_sem.at[0, star]),
            pltpu.make_async_copy(pull_ref.at[star], pull.at[star], load_sem.at[1, star]),
        )

    tables = [
        pltpu.make_async_copy(order_hbm, order_ref, table_sem.at[0]),
        pltpu.make_async_copy(map_hbm, map_ref, table_sem.at[1]),
    ]
    for copy in tables:
        copy.start()

    def start_load(star, _):
        for copy in load(star):
            copy.start()
        return 0

    lax.fori_loop(0, STARS, start_load, 0)

    barrier = pltpu.get_barrier_semaphore()

    def greet(target):
        pl.semaphore_signal(barrier, inc=1, device_id=target, device_id_type=MESH)

    def mix_target(o):
        return (zh + 1 - o // 16) % 2, (x + (o // 4) % 4) % 4, (y + o % 4) % 4

    def greet_mix(o, _):
        zh2, x2, y2 = mix_target(o)
        greet(device(zh2, x2, y2, zl, c))
        return 0

    def greet_direct(o, _):
        greet(device(zh, x, (y + o // 4) % 4, 2 * zz2 + (b + o // 2) % 2, (c + o) % 2))
        return 0

    def greet_mirror(o, _):
        greet(device(zz2, (x + o // 4) % 4, y, 2 * zh + (b + o // 2) % 2, (c + o) % 2))
        return 0

    lax.fori_loop(0, 16, greet_mix, 0)
    lax.fori_loop(17, 32, greet_mix, 0)
    lax.fori_loop(1, 16, greet_direct, 0)
    lax.fori_loop(1, 16, greet_mirror, 0)
    for step in (1, 7):
        greet(device((z + step) % 8 // 4, x, y, (z + step) % 4, c))

    @pl.when(zz2 != zh)
    def _():
        greet(device(zz2, x, y, 2 * zh + b, c))

    for copy in tables:
        copy.wait()
    row = lax.broadcasted_iota(jnp.int32, (FRAMES, FRAMES), 0)
    mode = (row // 8 % 2) * 128 + (row // 16) * 8 + row % 8
    local_sign = (1 - 2 * parity(mode & order_ref[...])).astype(F32).astype(BF16)

    def average(half, piece, first):
        def star_step(star, _):
            if first:
                for copy in load(star):
                    copy.wait()
                difference[star] = (push[star].astype(F32) - pull[star].astype(F32)).astype(BF16)
            columns = pl.ds(pl.multiple_of(half * HALF + piece * WIDTH, 128), WIDTH)
            index = map_ref[pl.ds(star, 1), columns] % SLOPES
            hot = (lax.broadcasted_iota(jnp.int32, (SLOPES, WIDTH), 0) == index).astype(F32).astype(BF16)
            total[...] += jnp.dot(difference[star], hot, preferred_element_type=F32)
            return 0

        total[...] = jnp.zeros_like(total)
        lax.fori_loop(0, STARS, star_step, 0)
        averaged = total[...] / STARS
        high = averaged.astype(BF16)
        low = (averaged - high.astype(F32)).astype(BF16)
        t = jnp.dot(local_sign, high, preferred_element_type=F32)
        t += jnp.dot(local_sign, low, preferred_element_type=F32)
        transformed[half, piece] = t.astype(BF16)

    def mix_copy(piece, o):
        zh2, x2, y2 = mix_target(o)
        rows = pl.multiple_of(16 * (4 * x2 + y2), 16)
        return remote(
            transformed.at[zh2, piece, pl.ds(rows, 16)],
            mixed.at[piece, pl.ds(pl.multiple_of(16 * poke, 16), 16)],
            mix_send.at[piece, o],
            mix_recv.at[piece, o],
            device(zh2, x2, y2, zl, c),
        )

    def start_mix(piece, lo, hi):
        lax.fori_loop(lo, hi, lambda o, _: (mix_copy(piece, o).start(), 0)[1], 0)

    def wait_mix(piece, lo, hi):
        lax.fori_loop(lo, hi, lambda o, _: (mix_copy(piece, o).wait(), 0)[1], 0)

    for piece in range(PIECES):
        average(1 - zh, piece, piece == 0)
        if piece == 0:
            pl.semaphore_wait(barrier, 31 + 15 + 15 + 2 + jnp.where(zz2 != zh, 1, 0))
        start_mix(piece, 0, 16)
        average(zh, piece, False)
        start_mix(piece, 17, 32)
        mixed[piece, pl.ds(pl.multiple_of(16 * poke, 16), 16), :] = transformed[
            zh, piece, pl.ds(pl.multiple_of(16 * (4 * x + y), 16), 16), :
        ]

    row = lax.broadcasted_iota(jnp.int32, (ROWS, ROWS), 0)
    col = lax.broadcasted_iota(jnp.int32, (ROWS, ROWS), 1)
    sign = 1 - 2 * parity((row % 32) & (col // 16))
    sign = jnp.where(row // 32 == col % 16, sign, 0).astype(F32).astype(BF16)

    def row_copy(piece, d):
        target = device(zh, x, (y + 4 - d) % 4, zl, c)
        return remote(
            row_block.at[0, piece],
            row_block.at[d, piece],
            gather_send.at[piece, d],
            gather_recv.at[piece, d],
            target,
        )

    def col_copy(piece, d):
        target = device(zh, (x + 4 - d) % 4, y, zl, c)
        return remote(
            col_block.at[0, piece],
            col_block.at[d, piece],
            gather_send.at[piece, 2 + d],
            gather_recv.at[piece, 2 + d],
            target,
        )

    near, far_col, far_row = [], [], []
    for piece in range(PIECES):
        wait_mix(piece, 0, 16)
        wait_mix(piece, 17, 32)
        demodulated = jnp.dot(sign, mixed[piece], preferred_element_type=F32)
        demodulated = (demodulated * (1.0 / math.sqrt(8192))).astype(BF16)
        row_block[0, piece] = demodulated
        col_block[0, piece] = demodulated
        for copy in (col_copy(piece, 1), row_copy(piece, 1), col_copy(piece, 3)):
            copy.start()
            near.append(copy)
    for piece in range(PIECES):
        far_col.append(col_copy(piece, 2))
        far_row.append(row_copy(piece, 2))
        far_col[-1].start()
        far_row[-1].start()

    def pick(core, tau):
        (dx0, dy0), (dx1, dy1) = BLOCKS[0][tau], BLOCKS[1][tau]
        return dx0 + core * (dx1 - dx0), dy0 + core * (dy1 - dy0)

    def block(core, tau):
        dx, dy = pick(core, tau)
        value = None
        for piece in range(PIECES):
            term = lax.dot_general(
                row_block[dy, piece],
                col_block[dx, piece],
                (((1,), (1,)), ((), ())),
                preferred_element_type=F32,
            )
            value = term if value is None else value + term
        return value

    def pair_copy(tau):
        return remote(
            pair_out.at[tau], pair_in.at[tau], pair_send.at[tau], pair_recv.at[tau], device(zh, x, y, zl, 1 - c)
        )

    def ring_copy(g, way, d, half):
        z2 = (z + (1 if way == 0 else 7)) % 8
        lo, hi = GROUPS[g]
        return remote(
            ring_out.at[way, d, half, lo:hi],
            ring_in.at[way, d, half, lo:hi],
            ring_send.at[g, way, d, half],
            ring_recv.at[g, way, d, half],
            device(z2 // 4, x, y, z2 % 4, c),
        )

    def ring_step(g, way, d, half, first=False):
        lo, hi = GROUPS[g]
        chunk = (z + (d if way == 0 else 8 - d)) % 8
        value = part[lo:hi, chunk, half * 64 : half * 64 + 64, :]
        if not first:
            ring_copy(g, way, d, half).wait_recv()
            value = value + ring_in[way, d, half, lo:hi].astype(F32)
        ring_out[way, d - 1, half, lo:hi] = value.astype(BF16)
        ring_copy(g, way, d - 1, half).start()

    def give(tau):
        pair_out[tau] = block(1 - c, tau).astype(BF16)
        pair_copy(tau).start()

    def keep(tau):
        value = block(c, tau)
        pair_copy(tau).wait_recv()
        value += pair_in[tau].astype(F32)
        for j in range(8):
            r, s = (j // 4) * 256 + (j % 2) * 128, (j // 2 % 2) * 256
            part[tau, j] = value[r : r + 128, s : s + 256]

    def begin(g):
        ring_step(g, 0, 4, 0, True)
        ring_step(g, 1, 4, 1, True)
        ring_step(g, 0, 3, 1, True)
        ring_step(g, 1, 3, 0, True)

    def progress(g, d):
        ring_step(g, 0, d, 0)
        ring_step(g, 1, d, 1)
        if d > 1:
            ring_step(g, 0, d - 1, 1)
            ring_step(g, 1, d - 1, 0)

    def is_here(target):
        return (target[0] == poke) & (target[1] == sensor)

    def ship(src, dst, send, recv, target):
        here = is_here(target)

        @pl.when(here)
        def _():
            pltpu.make_async_copy(src, dst, recv).start()

        @pl.when(jnp.logical_not(here))
        def _():
            remote(src, dst, send, recv, target).start()

    def shipped(src, dst, send, recv, target):
        @pl.when(jnp.logical_not(is_here(target)))
        def _():
            remote(src, dst, send, recv, target).wait_send()

    def direct(tau):
        dx, dy = pick(c, tau)
        i, j = (x + dx) % 4, (y + dy) % 4
        target = device(zh, x, j, 2 * zz2 + i // 2, i % 2)
        return final_out.at[0, tau], final_in.at[y, b], final_send.at[0, tau], final_recv.at[y, b], target

    def mirrored(tau):
        dx, dy = pick(c, tau)
        i, j = (x + dx) % 4, (y + dy) % 4
        target = device(zz2, i, y, 2 * zh + x // 2, x % 2)
        return final_out.at[1, tau], final_in.at[j, b], final_send.at[1, tau], final_recv.at[j, b], target

    def when_mirrored(tau, action):
        cores = [core for core in (0, 1) if is_mirrored(*BLOCKS[core][tau])]
        if len(cores) == 2:
            action()
        elif cores:
            pl.when(c == cores[0])(action)

    def finish(g):
        for way in (0, 1):
            for half in (0, 1):
                ring_copy(g, way, 0, half).wait_recv()
        for tau in range(*GROUPS[g]):
            value = part[tau, z] + ring_in[0, 0, :, tau].reshape(128, 256).astype(F32)
            value += ring_in[1, 0, :, tau].reshape(128, 256).astype(F32)
            value *= 1.0 / math.sqrt(8192)
            final_out[0, tau, 0] = value[:, :128].astype(SENT)
            final_out[0, tau, 1] = value[:, 128:].astype(SENT)
            ship(*direct(tau))

            def send_mirror(tau=tau, value=value):
                final_out[1, tau, 0] = value[:, :128].T.astype(SENT)
                final_out[1, tau, 1] = value[:, 128:].T.astype(SENT)
                ship(*mirrored(tau))

            when_mirrored(tau, send_mirror)

    for copy in near:
        copy.wait_recv()
    give(0)
    give(1)
    keep(0)
    begin(0)
    keep(1)
    begin(1)
    for d in (3, 2):
        progress(0, d)
        progress(1, d)
    for copy in far_col:
        copy.wait_recv()
    give(2)
    progress(0, 1)
    progress(1, 1)
    keep(2)
    begin(2)
    for copy in far_row:
        copy.wait_recv()
    give(3)
    give(4)
    finish(0)
    keep(3)
    begin(3)
    finish(1)
    keep(4)
    begin(4)
    for d in (3, 2, 1):
        for g in (2, 3, 4):
            progress(g, d)
    for g in (2, 3, 4):
        finish(g)

    for j in range(4):
        direct_in = is_computed((sensor - 4 * zz2 - x + 4) % 4, (y - j + 4) % 4)
        for half in range(2):
            pltpu.make_async_copy(final_out.at[0, 0], final_in.at[j, half], final_recv.at[j, half]).wait()
            for w in range(2):
                rows = half * direct_in + w * (1 - direct_in)
                cols = w * direct_in + half * (1 - direct_in)
                out_ref[
                    pl.ds(pl.multiple_of(rows * 128, 128), 128),
                    pl.ds(pl.multiple_of(j * 256 + cols * 128, 128), 128),
                ] = final_in[j, half, w].astype(F32)

    for copy in near + far_col + far_row:
        copy.wait_send()
    for g in range(len(GROUPS)):
        for d in (3, 2, 1, 0):
            for way in (0, 1):
                for half in (0, 1):
                    if d < 3 or way == half:
                        ring_copy(g, way, d, half).wait_send()
    for tau in range(KEPT):
        pair_copy(tau).wait_send()
        shipped(*direct(tau))
        when_mirrored(tau, lambda tau=tau: shipped(*mirrored(tau)))


def local(push_slopes, pull_slopes, pattern_order, star_map):
    dma = pltpu.SemaphoreType.DMA
    vmem = pl.BlockSpec(memory_space=pltpu.VMEM)
    hbm = pl.BlockSpec(memory_space=pl.ANY)
    return pl.pallas_call(
        demodulation_kernel,
        out_shape=jax.ShapeDtypeStruct((256, 1024), F32),
        in_specs=[hbm] * 4,
        out_specs=vmem,
        scratch_shapes=[
            pltpu.VMEM((STARS, FRAMES, SLOPES), BF16),
            pltpu.VMEM((STARS, FRAMES, SLOPES), BF16),
            pltpu.VMEM((1, FRAMES), jnp.int32),
            pltpu.VMEM((STARS, SLOPES), jnp.int32),
            pltpu.VMEM((STARS, FRAMES, SLOPES), BF16),
            pltpu.VMEM((FRAMES, WIDTH), F32),
            pltpu.VMEM((2, PIECES, FRAMES, WIDTH), BF16),
            pltpu.VMEM((PIECES, ROWS, WIDTH), BF16),
            pltpu.VMEM((3, PIECES, ROWS, WIDTH), BF16),
            pltpu.VMEM((4, PIECES, ROWS, WIDTH), BF16),
            pltpu.VMEM((KEPT, ROWS, ROWS), BF16),
            pltpu.VMEM((KEPT, ROWS, ROWS), BF16),
            pltpu.VMEM((KEPT, 8, 128, 256), F32),
            pltpu.VMEM((2, 4, 2, KEPT, 64, 256), BF16),
            pltpu.VMEM((2, 4, 2, KEPT, 64, 256), BF16),
            pltpu.VMEM((2, KEPT, 2, 128, 128), SENT),
            pltpu.VMEM((4, 2, 2, 128, 128), SENT),
            dma((2, STARS)),
            dma((2,)),
            dma((PIECES, 32)),
            dma((PIECES, 32)),
            dma((PIECES, 6)),
            dma((PIECES, 6)),
            dma((KEPT,)),
            dma((KEPT,)),
            dma((len(GROUPS), 2, 4, 2)),
            dma((len(GROUPS), 2, 4, 2)),
            dma((2, KEPT)),
            dma((4, 2)),
        ],
        compiler_params=pltpu.CompilerParams(
            collective_id=0, has_side_effects=True, vmem_limit_bytes=56 * 2**20
        ),
        name="demodulation",
    )(
        jnp.transpose(push_slopes, (1, 0, 2)),
        jnp.transpose(pull_slopes, (1, 0, 2)),
        pattern_order.reshape(1, -1),
        star_map,
    )


def solution(mesh):
    return jax.shard_map(
        local,
        mesh=mesh,
        in_specs=(P("poke", None, "sensor"), P("poke", None, "sensor"), P(), P(None, "sensor")),
        out_specs=P("poke", "sensor"),
        check_vma=False,
    )
```

time: 450 us -> 99.9 us (0.22)
  waiting for transfers between devices: 331 us -> 0 us
  Pallas kernels: 0 us -> 97.2 us
  blocking collectives: 41.8 us -> 0 us
  local copies, waits for them, and re-layouts: 34.8 us -> 2.31 us
  matrix products: 19.4 us -> 0 us
  between operations: 13.6 us -> 0.01 us
  other arithmetic: 5.81 us -> 0 us
    all_gather x1 -> x0, waiting for transfers between devices: 238 us -> none  [local(): lax.all_gather(demodulated, 'poke', axis=0, tiled=True)]
    pallas_call x0 -> x1, Pallas kernels: none -> 97.2 us  [local(): pl.pallas_call(demodulation_kernel, out_shape=jax.ShapeDtypeStruct((256,...]
    reduce_scatter x1 -> x0, waiting for transfers between devices: 92.9 us -> none  [local(): lax.psum_scatter(partial_value, 'sensor', scatter_dimension=1, tiled=True)]
    all_to_all x1 -> x0, blocking collectives: 41.8 us -> none  [local(): lax.all_to_all(stacked, 'poke', split_axis=1, concat_axis=0, tiled=True)]
    gather x6 -> x0, local copies, waits for them, and re-layouts: 26.7 us -> none  [the longest x5 21.7 us: star_average(): jnp.take(values[:, star_index, :], local_map[star_index], axis=1)]
    dot_general x3 -> x0, matrix products: 19.4 us -> none  [the longest x1 13.7 us: local(): lax.dot_general(demodulated, lax.all_gather(demodulated, 'poke', axis=0,...]
    unnamed x8 -> x1, local copies, waits for them, and re-layouts: 7.86 us -> 2.31 us
  transfers between devices with their start and end apart: 2 -> 0, of which waited for: 2 -> 0; matrix products, arithmetic and copies ran while one was open for 0% -> 0% of each run, Pallas kernels for 0% -> 0%
where the time goes in v2:
time: 99.9 us; the launch traced here: 99.6 us
  Pallas kernels  97.2 us (97%)
  local copies, waits for them, and re-layouts  2.31 us (2%)
    pallas_call x1, Pallas kernels, local(): pl.pallas_call(demodulation_kernel, out_shape=jax.ShapeDtypeStruct((256,...  97.2 us
    unnamed x1, local copies, waits for them, and re-layouts  2.31 us

profile of v2, /device:TPU:65, one launch (start us, length us, event | category | flops | bytes accessed | tf_op | source)
XLA Modules:
  0.0 99.6 jit_solution(11976810005975315811)
XLA Ops:
  0.0 97.2 %demodulation.1 = f32[256,1024]{1,0:T(8,128)} custom-call(bf16[6,256,1024]{2,1,0:T(8,128)(2,1)} %bitcast.3, bf16[6,256,1024]{2,1,0:T(8,128)(2,1)} %bitcast.4, s32[1,256]{1,0:T(1,128)} %bitcast.5, s32[6,1024]{1,0:T(8,128)} %map_hbm.1), custom_call_target="tpu_custom_call" | custom-call | tf_op jit(solution)/shard_map/demodulation/pallas_call | solution.py:431
  97.2 2.3 %copy.6 = f32[256,1024]{1,0:T(8,128)} copy(f32[256,1024]{1,0:T(8,128)} %demodulation.1) | data formatting | bytes 2097152

commit v3 on v2

--- a/solution.py
+++ b/solution.py
@@ -155,7 +155,8 @@
                     copy.wait()
                 difference[star] = (push[star].astype(F32) - pull[star].astype(F32)).astype(BF16)
             columns = pl.ds(pl.multiple_of(half * HALF + piece * WIDTH, 128), WIDTH)
-            index = map_ref[pl.ds(star, 1), columns] % SLOPES
+            index = jnp.where(lax.broadcasted_iota(jnp.int32, (STARS, WIDTH), 0) == star, map_ref[:, columns], 0)
+            index = jnp.sum(index, axis=0, keepdims=True) % SLOPES
             hot = (lax.broadcasted_iota(jnp.int32, (SLOPES, WIDTH), 0) == index).astype(F32).astype(BF16)
             total[...] += jnp.dot(difference[star], hot, preferred_element_type=F32)
             return 0
@@ -236,8 +237,6 @@
     for piece in range(PIECES):
         far_col.append(col_copy(piece, 2))
         far_row.append(row_copy(piece, 2))
-        far_col[-1].start()
-        far_row[-1].start()
 
     def pick(core, tau):
         (dx0, dy0), (dx1, dy1) = BLOCKS[0][tau], BLOCKS[1][tau]
@@ -366,6 +365,8 @@
 
     for copy in near:
         copy.wait_recv()
+    for copy in far_col + far_row:
+        copy.start()
     give(0)
     give(1)
     keep(0)

time: 99.9 us -> 89.7 us (0.90); the launches traced: 99.6 us -> 88.2 us
  Pallas kernels: 97.2 us -> 85.9 us
    pallas_call x1, Pallas kernels: 97.2 us -> 85.9 us  [local(): pl.pallas_call(demodulation_kernel, out_shape=jax.ShapeDtypeStruct((256,...]
where the time goes in v3:
time: 89.7 us; the launch traced here: 88.2 us
  Pallas kernels  85.9 us (96%)
  local copies, waits for them, and re-layouts  2.31 us (3%)
    pallas_call x1, Pallas kernels, local(): pl.pallas_call(demodulation_kernel, out_shape=jax.ShapeDtypeStruct((256,...  85.9 us
    unnamed x1, local copies, waits for them, and re-layouts  2.31 us

profile of v3, /device:TPU:65, one launch (start us, length us, event | category | flops | bytes accessed | tf_op | source)
XLA Modules:
  0.0 88.2 jit_solution(5397331637246511702)
XLA Ops:
  0.0 85.9 %demodulation.1 = f32[256,1024]{1,0:T(8,128)} custom-call(bf16[6,256,1024]{2,1,0:T(8,128)(2,1)} %bitcast.3, bf16[6,256,1024]{2,1,0:T(8,128)(2,1)} %bitcast.4, s32[1,256]{1,0:T(1,128)} %bitcast.5, s32[6,1024]{1,0:T(8,128)} %map_hbm.1), custom_call_target="tpu_custom_call" | custom-call | tf_op jit(solution)/shard_map/demodulation/pallas_call | solution.py:432
  85.9 2.3 %copy.6 = f32[256,1024]{1,0:T(8,128)} copy(f32[256,1024]{1,0:T(8,128)} %demodulation.1) | data formatting | bytes 2097152

commit v4 on v3

--- a/solution.py
+++ b/solution.py
@@ -59,6 +59,7 @@
     mixed,
     row_block,
     col_block,
+    relay,
     pair_out,
     pair_in,
     part,
@@ -203,25 +204,31 @@
     sign = 1 - 2 * parity((row % 32) & (col // 16))
     sign = jnp.where(row // 32 == col % 16, sign, 0).astype(F32).astype(BF16)
 
-    def row_copy(piece, d):
-        target = device(zh, x, (y + 4 - d) % 4, zl, c)
-        return remote(
-            row_block.at[0, piece],
-            row_block.at[d, piece],
-            gather_send.at[piece, d],
-            gather_recv.at[piece, d],
-            target,
-        )
-
-    def col_copy(piece, d):
-        target = device(zh, (x + 4 - d) % 4, y, zl, c)
-        return remote(
-            col_block.at[0, piece],
-            col_block.at[d, piece],
-            gather_send.at[piece, 2 + d],
-            gather_recv.at[piece, 2 + d],
-            target,
-        )
+    def gather(src, dst, piece, k, dx, dy):
+        target = device(zh, (x + dx) % 4, (y + dy) % 4, zl, c)
+        return remote(src, dst, gather_send.at[piece, k], gather_recv.at[piece, k], target)
+
+    low, high = pl.ds(0, ROWS // 2), pl.ds(ROWS // 2, ROWS // 2)
+
+    def near_copies(piece):
+        return [
+            gather(col_block.at[0, piece], col_block.at[1, piece], piece, 0, 3, 0),
+            gather(row_block.at[0, piece], row_block.at[1, piece], piece, 1, 0, 3),
+            gather(col_block.at[0, piece], col_block.at[3, piece], piece, 2, 1, 0),
+            gather(row_block.at[0, piece, high], relay.at[piece], piece, 3, 0, 1),
+        ]
+
+    def far_col_copies(piece):
+        return [
+            gather(col_block.at[1, piece, low], col_block.at[2, piece, low], piece, 4, 3, 0),
+            gather(col_block.at[3, piece, high], col_block.at[2, piece, high], piece, 5, 1, 0),
+        ]
+
+    def far_row_copies(piece):
+        return [
+            gather(row_block.at[1, piece, low], row_block.at[2, piece, low], piece, 6, 0, 3),
+            gather(relay.at[piece], row_block.at[2, piece, high], piece, 7, 0, 1),
+        ]
 
     near, far_col, far_row = [], [], []
     for piece in range(PIECES):
@@ -231,12 +238,12 @@
         demodulated = (demodulated * (1.0 / math.sqrt(8192))).astype(BF16)
         row_block[0, piece] = demodulated
         col_block[0, piece] = demodulated
-        for copy in (col_copy(piece, 1), row_copy(piece, 1), col_copy(piece, 3)):
+        for copy in near_copies(piece):
             copy.start()
             near.append(copy)
     for piece in range(PIECES):
-        far_col.append(col_copy(piece, 2))
-        far_row.append(row_copy(piece, 2))
+        far_col += far_col_copies(piece)
+        far_row += far_row_copies(piece)
 
     def pick(core, tau):
         (dx0, dy0), (dx1, dy1) = BLOCKS[0][tau], BLOCKS[1][tau]
@@ -409,7 +416,7 @@
                 out_ref[
                     pl.ds(pl.multiple_of(rows * 128, 128), 128),
                     pl.ds(pl.multiple_of(j * 256 + cols * 128, 128), 128),
-                ] = final_in[j, half, w].astype(F32)
+                ] = final_in[j, half, w]
 
     for copy in near + far_col + far_row:
         copy.wait_send()
@@ -431,7 +438,7 @@
     hbm = pl.BlockSpec(memory_space=pl.ANY)
     return pl.pallas_call(
         demodulation_kernel,
-        out_shape=jax.ShapeDtypeStruct((256, 1024), F32),
+        out_shape=jax.ShapeDtypeStruct((256, 1024), SENT),
         in_specs=[hbm] * 4,
         out_specs=vmem,
         scratch_shapes=[
@@ -445,6 +452,7 @@
             pltpu.VMEM((PIECES, ROWS, WIDTH), BF16),
             pltpu.VMEM((3, PIECES, ROWS, WIDTH), BF16),
             pltpu.VMEM((4, PIECES, ROWS, WIDTH), BF16),
+            pltpu.VMEM((PIECES, ROWS // 2, WIDTH), BF16),
             pltpu.VMEM((KEPT, ROWS, ROWS), BF16),
             pltpu.VMEM((KEPT, ROWS, ROWS), BF16),
             pltpu.VMEM((KEPT, 8, 128, 256), F32),
@@ -456,8 +464,8 @@
             dma((2,)),
             dma((PIECES, 32)),
             dma((PIECES, 32)),
-            dma((PIECES, 6)),
-            dma((PIECES, 6)),
+            dma((PIECES, 8)),
+            dma((PIECES, 8)),
             dma((KEPT,)),
             dma((KEPT,)),
             dma((len(GROUPS), 2, 4, 2)),
@@ -474,7 +482,7 @@
         jnp.transpose(pull_slopes, (1, 0, 2)),
         pattern_order.reshape(1, -1),
         star_map,
-    )
+    ).astype(F32)
 
 
 def solution(mesh):

time: 89.7 us -> 88.4 us (0.986); the launches traced: 88.2 us -> 88.1 us
  local copies, waits for them, and re-layouts: 2.31 us -> 0 us
  other arithmetic: 0 us -> 2.13 us
    unnamed x1 -> x0, local copies, waits for them, and re-layouts: 2.31 us -> none
    convert_element_type x0 -> x1, other arithmetic: none -> 2.13 us  [local(): return pl.pallas_call(demodulation_kernel, out_shape=jax.ShapeDtypeStruct...]
where the time goes in v4:
time: 88.4 us; the launch traced here: 88.1 us
  Pallas kernels  86 us (97%)
  other arithmetic  2.13 us (2%)
    pallas_call x1, Pallas kernels, local(): pl.pallas_call(demodulation_kernel, out_shape=jax.ShapeDtypeStruct((256,...  86 us
    convert_element_type x1, other arithmetic, local(): return pl.pallas_call(demodulation_kernel, out_shape=jax.ShapeDtypeStruct...  2.13 us

profile of v4, /device:TPU:65, one launch (start us, length us, event | category | flops | bytes accessed | tf_op | source)
XLA Modules:
  0.0 88.1 jit_solution(2147933296116602033)
XLA Ops:
  0.0 86.0 %demodulation.1 = bf16[256,1024]{1,0:T(8,128)(2,1)} custom-call(bf16[6,256,1024]{2,1,0:T(8,128)(2,1)} %bitcast.3, bf16[6,256,1024]{2,1,0:T(8,128)(2,1)} %bitcast.4, s32[1,256]{1,0:T(1,128)} %bitcast.5, s32[6,1024]{1,0:T(8,128)} %map_hbm.1), custom_call_target="tpu_custom_call" | custom-call | tf_op jit(solution)/shard_map/demodulation/pallas_call | solution.py:439
  86.0 2.1 %convert_element_type.3 = f32[256,1024]{1,0:T(8,128)} convert(bf16[256,1024]{1,0:T(8,128)(2,1)} %demodulation.1) | non-fusion elementwise | flops 262144 | bytes 1572864 | tf_op jit(solution)/shard_map/convert_element_type | solution.py:485

commit v5 on v4

--- a/solution.py
+++ b/solution.py
@@ -380,31 +380,37 @@
     begin(0)
     keep(1)
     begin(1)
-    for d in (3, 2):
-        progress(0, d)
-        progress(1, d)
-    for copy in far_col:
+    progress(0, 3)
+    progress(1, 3)
+    for copy in far_col + far_row:
         copy.wait_recv()
     give(2)
+    give(3)
+    give(4)
+    keep(2)
+    begin(2)
+    progress(0, 2)
+    progress(1, 2)
+    keep(3)
+    begin(3)
     progress(0, 1)
     progress(1, 1)
-    keep(2)
-    begin(2)
-    for copy in far_row:
-        copy.wait_recv()
-    give(3)
-    give(4)
-    finish(0)
-    keep(3)
-    begin(3)
-    finish(1)
     keep(4)
     begin(4)
-    for d in (3, 2, 1):
-        for g in (2, 3, 4):
-            progress(g, d)
-    for g in (2, 3, 4):
-        finish(g)
+    progress(2, 3)
+    progress(3, 3)
+    progress(4, 3)
+    progress(2, 2)
+    progress(3, 2)
+    progress(4, 2)
+    progress(2, 1)
+    progress(3, 1)
+    progress(4, 1)
+    finish(0)
+    finish(1)
+    finish(2)
+    finish(3)
+    finish(4)
 
     for j in range(4):
         direct_in = is_computed((sensor - 4 * zz2 - x + 4) % 4, (y - j + 4) % 4)

time: 88.4 us -> 88.4 us (level)
  no operation moved by 1% of the time
where the time goes in v5:
time: 88.4 us; the launch traced here: 88.3 us
  Pallas kernels  86.2 us (98%)
  other arithmetic  2.13 us (2%)
    pallas_call x1, Pallas kernels, local(): pl.pallas_call(demodulation_kernel, out_shape=jax.ShapeDtypeStruct((256,...  86.2 us
    convert_element_type x1, other arithmetic, local(): return pl.pallas_call(demodulation_kernel, out_shape=jax.ShapeDtypeStruct...  2.13 us

profile of v5, /device:TPU:65, one launch (start us, length us, event | category | flops | bytes accessed | tf_op | source)
XLA Modules:
  0.0 88.3 jit_solution(3274297778226146504)
XLA Ops:
  0.0 86.2 %demodulation.1 = bf16[256,1024]{1,0:T(8,128)(2,1)} custom-call(bf16[6,256,1024]{2,1,0:T(8,128)(2,1)} %bitcast.3, bf16[6,256,1024]{2,1,0:T(8,128)(2,1)} %bitcast.4, s32[1,256]{1,0:T(1,128)} %bitcast.5, s32[6,1024]{1,0:T(8,128)} %map_hbm.1), custom_call_target="tpu_custom_call" | custom-call | tf_op jit(solution)/shard_map/demodulation/pallas_call | solution.py:445
  86.2 2.1 %convert_element_type.3 = f32[256,1024]{1,0:T(8,128)} convert(bf16[256,1024]{1,0:T(8,128)(2,1)} %demodulation.1) | non-fusion elementwise | flops 262144 | bytes 1572864 | tf_op jit(solution)/shard_map/convert_element_type | solution.py:491
